TPU v7x, 32 devices: a whole 2x2x4 slice. The times are simulated.
32 devices in a mesh: grp: 8 (over y, x, core), rep: 4 (over z).
Axes of the slice: x: 2, y: 2, z: 4, core: 2. Of those that a mesh axis runs over, the one named last changes fastest.
Arguments:
- layer_input: bfloat16 [4, 2048, 2048], P('rep', 'grp'), may hold values from -6 to 6
- cotangent: bfloat16 [4, 2048, 2048], P('rep', 'grp'), may hold values from -6 to 6
- cut_order: int32 [4, 16], P('rep'), may hold values from 0 to 15, each once within a row
- piece_ids: int32 [4, 2048], P('rep'), may hold values from 0 to 8, as said below
- w_query: bfloat16 [2048, 2048], P('grp'), may hold values from -0.1875 to 0.1875
- w_key: bfloat16 [2048, 1024], P('grp'), may hold values from -0.1875 to 0.1875
- w_value: bfloat16 [2048, 1024], P('grp'), may hold values from -0.125 to 0.125
- w_out: bfloat16 [2048, 2048], P('grp'), may hold values from -0.5 to 0.5
- w_gate: bfloat16 [2048, 8192], P('grp'), may hold values from -0.125 to 0.125
- w_up: bfloat16 [2048, 8192], P('grp'), may hold values from -0.125 to 0.125
- w_down: bfloat16 [8192, 2048], P('grp'), may hold values from -0.125 to 0.125
- gain_attn: float32 [2048], replicated, may hold values from 0.25 to 1.75
- gain_ffn: float32 [2048], replicated, may hold values from 0.25 to 1.75
Outputs:
- layer_output: bfloat16 [4, 2048, 2048], P('rep', 'grp')
- grad_x: bfloat16 [4, 2048, 2048], P('rep', 'grp')
- grad_w_query: float32 [2048, 2048], P('grp')
- grad_w_key: float32 [2048, 1024], P('grp')
- grad_w_value: float32 [2048, 1024], P('grp')
- grad_w_out: float32 [2048, 2048], P('grp')
- grad_w_gate: float32 [2048, 8192], P('grp')
- grad_w_up: float32 [2048, 8192], P('grp')
- grad_w_down: float32 [8192, 2048], P('grp')
- grad_gain_attn: float32 [2048], P('grp')
- grad_gain_ffn: float32 [2048], P('grp')
Inputs may be any that keep to these rules, and one draw needn't show every extreme that they name: `cut_order`: each row is a permutation of the 16 cut numbers. `piece_ids`: A sequence is cut into aligned runs of 256 positions; run k carries id k + 1 on all its positions if it is a picture, else 0; the last run of every sequence is a picture.
All inputs are finite; a program needn't handle non-finite values.
Results may differ from a plain program's by a relative error of at most 0.024.
Values may be sent and summed in bfloat16 or wider, within the bound.
A program may use at most 640 MiB of HBM per device.

v0:
```python
import jax
import jax.numpy as jnp
from jax import lax
from jax.sharding import PartitionSpec as P

HD = 128
EPS = 1e-05
ROPE_BASE = 1000000.0


def matmul_f32(first, second):
    return jnp.dot(first, second, preferred_element_type=jnp.float32)


def against_rows(first, second):
    return jnp.einsum("tc,rc->tr", first, second, preferred_element_type=jnp.float32)


def over_tokens(first, second):
    return jnp.einsum("tr,tc->rc", first, second, preferred_element_type=jnp.float32)


def turn_tables(places, head_size):
    half_size = head_size // 2
    inverse = ROPE_BASE ** (-(jnp.arange(half_size, dtype=jnp.float32) * 2.0) / head_size)
    angles = places.astype(jnp.float32)[..., None] * inverse
    cosine = jnp.concatenate([jnp.cos(angles), jnp.cos(angles)], -1)[:, :, None, :]
    sine_table = jnp.concatenate([jnp.sin(angles), jnp.sin(angles)], -1)[:, :, None, :]
    return (cosine, sine_table)


def rotate(features, cosine, sine_table):
    half_size = features.shape[-1] // 2
    turned = jnp.concatenate([-features[..., half_size:], features[..., :half_size]], -1)
    return features * cosine + turned * sine_table


def rotate_back(incoming, cosine, sine_table):
    half_size = incoming.shape[-1] // 2
    scaled = incoming * sine_table
    return incoming * cosine + jnp.concatenate(
        [scaled[..., half_size:], -scaled[..., :half_size]], -1
    )


def norm_back(upstream, grad_normed, unit_rows, inv_root, gain):
    scaled = grad_normed * gain
    center_term = jnp.mean(scaled * unit_rows, -1, keepdims=True)
    return (
        upstream + inv_root * (scaled - unit_rows * center_term),
        jnp.sum(grad_normed * unit_rows, 0),
    )


def seven_terms(
    normed_cols,
    attended_cols,
    second_cols,
    hidden_cols,
    grads,
    row_count,
    hidden_ratio,
    model_width,
):
    grad_query, grad_key, grad_value, grad_mid_low, grad_gate, grad_up, grad_out = grads
    return jnp.concatenate(
        [
            over_tokens(normed_cols, grad_query),
            over_tokens(normed_cols, grad_key),
            over_tokens(normed_cols, grad_value),
            over_tokens(attended_cols, grad_mid_low),
            over_tokens(second_cols, grad_gate),
            over_tokens(second_cols, grad_up),
            over_tokens(hidden_cols, grad_out).reshape(row_count, hidden_ratio * model_width),
        ],
        1,
    )


def on_device(
    layer_input,
    cotangent,
    cut_order,
    piece_ids,
    w_query,
    w_key,
    w_value,
    w_out,
    w_gate,
    w_up,
    w_down,
    gain_attn,
    gain_ffn,
):
    groups = lax.axis_size("grp")
    own_index = lax.axis_index("grp")
    seq_count, local_rows, model_width = layer_input.shape
    length = piece_ids.shape[1]
    cut_len = length // cut_order.shape[1]
    token_count = seq_count * local_rows
    q_width = w_query.shape[1]
    kv_width = w_key.shape[1]
    head_count = q_width // HD
    kv_heads = kv_width // HD
    group_size = head_count // kv_heads
    hidden_width = w_gate.shape[1]
    hidden_ratio = hidden_width // model_width
    score_scale = HD ** (-0.5)
    key_block = min(512, length)
    blocks = length // key_block
    rows_here = model_width // groups
    f32 = jnp.float32
    bf16 = jnp.bfloat16
    rows_all = jnp.arange(length, dtype=jnp.int32)
    slot_of_row = jnp.broadcast_to(rows_all // cut_len, (seq_count, length))
    key_places = jnp.take_along_axis(cut_order, slot_of_row, axis=1) * cut_len + rows_all % cut_len
    key_pieces = jnp.take_along_axis(piece_ids, key_places, axis=1)
    query_places = lax.dynamic_slice_in_dim(key_places, own_index * local_rows, local_rows, 1)
    query_pieces = lax.dynamic_slice_in_dim(key_pieces, own_index * local_rows, local_rows, 1)
    cosine, sine_table = turn_tables(query_places, HD)
    x_flat = layer_input.reshape(token_count, model_width).astype(f32)
    inv_one = lax.rsqrt(jnp.mean(x_flat * x_flat, -1, keepdims=True) + EPS)
    unit_one = x_flat * inv_one
    normed_one = (unit_one * gain_attn).astype(bf16)
    rows_query = lax.all_gather(w_query, "grp", axis=0, tiled=True)
    rows_key = lax.all_gather(w_key, "grp", axis=0, tiled=True)
    rows_value = lax.all_gather(w_value, "grp", axis=0, tiled=True)
    rows_out = lax.all_gather(w_out, "grp", axis=0, tiled=True)
    columns = normed_one
    query_lin = matmul_f32(columns, rows_query)
    key_lin = matmul_f32(columns, rows_key)
    value_lin = matmul_f32(columns, rows_value)
    out_full = rows_out
    query_turned = rotate(
        query_lin.reshape(seq_count, local_rows, head_count, HD), cosine, sine_table
    ).astype(bf16)
    key_turned = rotate(
        key_lin.reshape(seq_count, local_rows, kv_heads, HD), cosine, sine_table
    ).astype(bf16)
    value_local = value_lin.astype(bf16).reshape(seq_count, local_rows, kv_width)
    key_all, value_all = (
        lax.all_gather(
            key_turned.reshape(seq_count, local_rows, kv_width), "grp", axis=1, tiled=True
        ),
        lax.all_gather(value_local, "grp", axis=1, tiled=True),
    )
    query_grouped = query_turned.reshape(seq_count, local_rows, kv_heads, group_size, HD)

    def block_keys(step_index):
        first_row = step_index * key_block
        key_rows = lax.dynamic_slice_in_dim(key_all, first_row, key_block, 1).reshape(
            seq_count, key_block, kv_heads, HD
        )
        value_rows = lax.dynamic_slice_in_dim(value_all, first_row, key_block, 1).reshape(
            seq_count, key_block, kv_heads, HD
        )
        block_places = lax.dynamic_slice_in_dim(key_places, first_row, key_block, 1)
        block_pieces = lax.dynamic_slice_in_dim(key_pieces, first_row, key_block, 1)
        allowed = (block_places[:, None, :] <= query_places[:, :, None]) | (
            query_pieces[:, :, None] != 0
        ) & (block_pieces[:, None, :] == query_pieces[:, :, None])
        return (key_rows, value_rows, allowed)

    def scores_of(key_rows, allowed):
        raw_scores = (
            jnp.einsum("sqkgd,snkd->skgqn", query_grouped, key_rows, preferred_element_type=f32)
            * score_scale
        )
        return jnp.where(allowed[:, None, None], raw_scores, -1e30)

    stat_shape = (seq_count, kv_heads, group_size, local_rows)

    def extent(step_index, state_now):
        running_max, running_sum = state_now
        key_rows, value_rows, allowed = block_keys(step_index)
        scores = scores_of(key_rows, allowed)
        new_max = jnp.maximum(running_max, jnp.max(scores, -1))
        running_sum = running_sum * jnp.exp(running_max - new_max) + jnp.sum(
            jnp.exp(scores - new_max[..., None]), -1
        )
        return (new_max, running_sum)

    running_max, running_sum = lax.fori_loop(
        0, blocks, extent, (jnp.full(stat_shape, -1e30, f32), jnp.zeros(stat_shape, f32))
    )
    log_total = running_max + jnp.log(running_sum)

    def weigh(step_index, accum):
        key_rows, value_rows, allowed = block_keys(step_index)
        probabilities = jnp.exp(scores_of(key_rows, allowed) - log_total[..., None]).astype(bf16)
        return accum + jnp.einsum(
            "skgqn,snkd->sqkgd", probabilities, value_rows, preferred_element_type=f32
        )

    mixed_heads = lax.fori_loop(
        0, blocks, weigh, jnp.zeros((seq_count, local_rows, kv_heads, group_size, HD), f32)
    )
    attended = mixed_heads.reshape(token_count, q_width).astype(bf16)
    residual_mid = x_flat + matmul_f32(attended, out_full)
    inv_two = lax.rsqrt(jnp.mean(residual_mid * residual_mid, -1, keepdims=True) + EPS)
    unit_two = residual_mid * inv_two
    normed_two = (unit_two * gain_ffn).astype(bf16)
    rows_gate = lax.all_gather(w_gate, "grp", axis=0, tiled=True)
    rows_up = lax.all_gather(w_up, "grp", axis=0, tiled=True)
    columns = normed_two
    gate_proj = matmul_f32(columns, rows_gate)
    up_proj = matmul_f32(columns, rows_up)
    sigmoid_gate = jax.nn.sigmoid(gate_proj)
    swish = gate_proj * sigmoid_gate
    hidden = (swish * up_proj).astype(bf16)
    columns = hidden
    ffn_out = matmul_f32(columns, lax.all_gather(w_down, "grp", axis=0, tiled=True))
    result = (residual_mid + ffn_out).astype(bf16).reshape(seq_count, local_rows, model_width)
    grad_out = cotangent.reshape(token_count, model_width)
    grad_flat = grad_out.astype(f32)
    grad_hidden = jnp.einsum(
        "td,fd->tf",
        grad_out,
        lax.all_gather(w_down, "grp", axis=0, tiled=True),
        preferred_element_type=f32,
    )
    grad_gate = (
        grad_hidden * up_proj * sigmoid_gate * (1.0 + gate_proj * (1.0 - sigmoid_gate))
    ).astype(bf16)
    grad_up = (grad_hidden * swish).astype(bf16)
    rows_gate = lax.all_gather(w_gate, "grp", axis=0, tiled=True)
    rows_up = lax.all_gather(w_up, "grp", axis=0, tiled=True)
    rows_out = lax.all_gather(w_out, "grp", axis=0, tiled=True)
    row_term = against_rows(grad_gate, rows_gate) + against_rows(grad_up, rows_up)
    grad_two = row_term
    grad_mid, gain_ffn_term = norm_back(grad_flat, grad_two, unit_two, inv_two, gain_ffn)
    grad_mid_low = grad_mid.astype(bf16)
    grad_attended = against_rows(grad_mid_low, rows_out).astype(bf16)
    grad_grouped = grad_attended.reshape(seq_count, local_rows, kv_heads, group_size, HD)

    def spread(step_index, accum):
        key_rows, value_rows, allowed = block_keys(step_index)
        probabilities = jnp.exp(scores_of(key_rows, allowed) - log_total[..., None])
        prob_grad = jnp.einsum(
            "sqkgd,snkd->skgqn", grad_grouped, value_rows, preferred_element_type=f32
        )
        return accum + jnp.sum(probabilities * prob_grad, -1)

    center = lax.fori_loop(0, blocks, spread, jnp.zeros(stat_shape, f32))

    def back_block(step_index, state_now):
        grad_query, grad_keys, grad_values = state_now
        key_rows, value_rows, allowed = block_keys(step_index)
        probabilities = jnp.exp(scores_of(key_rows, allowed) - log_total[..., None])
        prob_grad = jnp.einsum(
            "sqkgd,snkd->skgqn", grad_grouped, value_rows, preferred_element_type=f32
        )
        grad_scores = (probabilities * (prob_grad - center[..., None])).astype(bf16)
        grad_query = grad_query + score_scale * jnp.einsum(
            "skgqn,snkd->sqkgd", grad_scores, key_rows, preferred_element_type=f32
        )
        key_term = score_scale * jnp.einsum(
            "skgqn,sqkgd->snkd", grad_scores, query_grouped, preferred_element_type=f32
        )
        value_term = jnp.einsum(
            "skgqn,sqkgd->snkd",
            probabilities.astype(bf16),
            grad_grouped,
            preferred_element_type=f32,
        )
        first_row = step_index * key_block
        grad_keys = lax.dynamic_update_slice_in_dim(
            grad_keys, key_term.reshape(seq_count, key_block, kv_width), first_row, 1
        )
        grad_values = lax.dynamic_update_slice_in_dim(
            grad_values, value_term.reshape(seq_count, key_block, kv_width), first_row, 1
        )
        return (grad_query, grad_keys, grad_values)

    back_start = (
        jnp.zeros((seq_count, local_rows, kv_heads, group_size, HD), f32),
        jnp.zeros((seq_count, length, kv_width), f32),
        jnp.zeros((seq_count, length, kv_width), f32),
    )
    grad_query_turned, grad_keys_all, grad_values_all = lax.fori_loop(
        0, blocks, back_block, back_start
    )
    grad_keys_own, grad_values_own = (
        lax.psum_scatter(
            grad_keys_all.astype(jnp.bfloat16), "grp", scatter_dimension=1, tiled=True
        ).astype(jnp.float32),
        lax.psum_scatter(
            grad_values_all.astype(jnp.bfloat16), "grp", scatter_dimension=1, tiled=True
        ).astype(jnp.float32),
    )
    grad_query = (
        rotate_back(
            grad_query_turned.reshape(seq_count, local_rows, head_count, HD), cosine, sine_table
        )
        .astype(bf16)
        .reshape(token_count, q_width)
    )
    grad_key = (
        rotate_back(grad_keys_own.reshape(seq_count, local_rows, kv_heads, HD), cosine, sine_table)
        .astype(bf16)
        .reshape(token_count, kv_width)
    )
    grad_value = grad_values_own.astype(bf16).reshape(token_count, kv_width)
    rows_query = lax.all_gather(w_query, "grp", axis=0, tiled=True)
    rows_key = lax.all_gather(w_key, "grp", axis=0, tiled=True)
    rows_value = lax.all_gather(w_value, "grp", axis=0, tiled=True)
    row_term = (
        against_rows(grad_query, rows_query)
        + against_rows(grad_key, rows_key)
        + against_rows(grad_value, rows_value)
    )
    grad_input, gain_attn_term = norm_back(grad_mid, row_term, unit_one, inv_one, gain_attn)
    grad_x = grad_input.astype(bf16).reshape(seq_count, local_rows, model_width)
    token_grads = (grad_query, grad_key, grad_value, grad_mid_low, grad_gate, grad_up, grad_out)
    grad_shard = lax.psum_scatter(
        seven_terms(
            normed_one,
            attended,
            normed_two,
            hidden,
            token_grads,
            rows_here * lax.axis_size("grp"),
            hidden_ratio,
            model_width,
        ).astype(jnp.bfloat16),
        "grp",
        scatter_dimension=0,
        tiled=True,
    ).astype(jnp.float32)
    grad_shard = lax.psum(grad_shard.astype(jnp.bfloat16), "rep").astype(jnp.float32)
    gain_total = lax.psum(jnp.stack([gain_attn_term, gain_ffn_term]), ("grp", "rep"))
    own_gains = lax.dynamic_slice_in_dim(gain_total, own_index * rows_here, rows_here, 1)
    widths = [q_width, kv_width, kv_width, model_width, hidden_width, hidden_width, hidden_width]
    offsets = [0]
    for column_count in widths:
        offsets.append(offsets[-1] + column_count)
    split_grads = [
        grad_shard[:, offsets[number] : offsets[number + 1]] for number in range(len(widths))
    ]
    grad_down = split_grads[6].reshape(rows_here * hidden_ratio, model_width)
    return (
        result,
        grad_x,
        split_grads[0],
        split_grads[1],
        split_grads[2],
        split_grads[3],
        split_grads[4],
        split_grads[5],
        grad_down,
        own_gains[0],
        own_gains[1],
    )


def solution(mesh):
    in_specs = (
        P("rep", "grp", None),
        P("rep", "grp", None),
        P("rep", None),
        P("rep", None),
        P("grp", None),
        P("grp", None),
        P("grp", None),
        P("grp", None),
        P("grp", None),
        P("grp", None),
        P("grp", None),
        P(),
        P(),
    )
    out_specs = (
        P("rep", "grp", None),
        P("rep", "grp", None),
        P("grp", None),
        P("grp", None),
        P("grp", None),
        P("grp", None),
        P("grp", None),
        P("grp", None),
        P("grp", None),
        P("grp"),
        P("grp"),
    )
    return jax.shard_map(
        on_device, mesh=mesh, in_specs=in_specs, out_specs=out_specs, check_vma=False
    )
```

profile of v0, /device:TPU:0, one launch (start us, length us, event | category | flops | bytes accessed | tf_op | source)
XLA Modules:
  0.0 2414.0 jit_solution(6027990927874666065)
XLA Ops:
  10.3 39.1 %all-gather.12.cloned.1.call-done = bf16[2048,1024]{1,0:T(8,128)(2,1)} async-done(((bf16[256,1024]{1,0:T(8,128)(2,1)}), bf16[2048,1024]{1,0:T(8,128)(2,1)}) %all-gather.12.cloned.1.call-update) | async-done | bytes 4194320 | tf_op jit(solution)/shard_map/all_gather | solution.py:127
  59.7 5.5 select_select_fusion
  65.2 11.8 gather_fusion
  77.7 10.3 all-gather.14.cloned.1.call-done
  98.6 28.6 %all-gather.26.cloned.1.call-done = bf16[2048,1024]{1,0:T(8,128)(2,1)} async-done(((bf16[256,1024]{1,0:T(8,128)(2,1)}), bf16[2048,1024]{1,0:T(8,128)(2,1)}) %all-gather.26.cloned.1.call-update) | async-done | bytes 4194320 | tf_op jit(solution)/shard_map/all_gather | solution.py:145
  127.2 6.4 copy.139
  133.6 32.6 %all-gather.28.cloned.1.call-done = bf16[2048,1024]{1,0:T(8,128)(2,1)} async-done(((bf16[256,1024]{1,0:T(8,128)(2,1)}), bf16[2048,1024]{1,0:T(8,128)(2,1)}) %all-gather.28.cloned.1.call-update) | async-done | bytes 4194320 | tf_op jit(solution)/shard_map/all_gather | solution.py:142
  166.3 6.5 copy.140
  172.8 49.6 %all-gather.16.cloned.1.call-done = bf16[2048,2048]{1,0:T(8,128)(2,1)} async-done(((bf16[256,2048]{1,0:T(8,128)(2,1)}), bf16[2048,2048]{1,0:T(8,128)(2,1)}) %all-gather.16.cloned.1.call-update) | async-done | bytes 8388624 | tf_op jit(solution)/shard_map/all_gather | solution.py:125
  222.5 7.1 fusion.95
  231.1 47.8 %while.62 = (s32[]{:T(128)}, f32[1,8,2,256]{3,2,1,0:T(2,128)S(1)}, f32[1,8,2,256]{3,2,1,0:T(2,128)S(1)}, s32[1,2048]{1,0:T(1,128)S(1)}, s32[1,256]{1,0:T(1,128)S...) while((s32[]{:T(128)}, f32[1,8,2,256]{3,2,1,0:T(2,128)S(1)}, ...), condition=%wide.region_4.5_spmd.clone, body=%wide.region_1.4_spmd.clone.sunk | while | flops 552096000 | bytes 21593796 | solution.py:183
  249.5 5.8 exponential_reduce_fusion.2
  278.9 36.6 %while.63 = (s32[]{:T(128)}, f32[1,256,8,2,128]{1,4,3,2,0:T(8,128)}, bf16[1,2048,1024]{1,2,0:T(8,128)(2,1)}, s32[1,2048]{1,0:T(1,128)S(1)}, s32[1,256]{1,0:T(1,1...) while((s32[]{:T(128)}, ...), condition=%wide.region_6.7_spmd.clone, body=%wide.region_5.6_spmd.clone.sunk | while | flops 1083703552 | bytes 11828941 | solution.py:195
  290.6 6.6 bitcast_add_fusion.10
  300.1 6.1 bitcast_add_fusion.10
  309.1 6.1 bitcast_add_fusion.10
  317.3 6.2 multiply_reduce_fusion.2
  325.1 116.2 %all-gather.20.cloned.1.call-done = bf16[2048,8192]{1,0:T(8,128)(2,1)} async-done(((bf16[256,8192]{1,0:T(8,128)(2,1)}), bf16[2048,8192]{1,0:T(8,128)(2,1)}) %all-gather.20.cloned.1.call-update) | async-done | bytes 33554448 | tf_op jit(solution)/shard_map/all_gather | solution.py:203
  441.3 20.2 fusion.109
  461.5 142.5 %all-gather.22.cloned.1.call-done = bf16[2048,8192]{1,0:T(8,128)(2,1)} async-done(((bf16[256,8192]{1,0:T(8,128)(2,1)}), bf16[2048,8192]{1,0:T(8,128)(2,1)}) %all-gather.22.cloned.1.call-update) | async-done | bytes 33554448 | tf_op jit(solution)/shard_map/all_gather | solution.py:204
  604.0 20.2 fusion.110
  624.2 142.5 %all-gather.24.cloned.1.call-done = bf16[8192,2048]{1,0:T(8,128)(2,1)} async-done(((bf16[1024,2048]{1,0:T(8,128)(2,1)}), bf16[8192,2048]{1,0:T(8,128)(2,1)}) %all-gather.24.cloned.1.call-update) | async-done | bytes 33554448 | tf_op jit(solution)/shard_map/all_gather | solution.py:212
  766.8 23.2 multiply_convert_fusion
  790.0 17.0 fusion.111
  807.0 18.8 multiply_reduce_fusion
  829.6 5.8 convolution_convert_fusion.5
  838.6 24.8 %while.64 = (s32[]{:T(128)}, f32[1,8,2,256]{3,2,1,0:T(2,128)S(1)}, s32[1,2048]{1,0:T(1,128)S(1)}, s32[1,256]{1,0:T(1,128)S(1)}, s32[1,256]{1,0:T(1,128)S(1)}, /*...) while((s32[]{:T(128)}, f32[1,8,2,256]{3,2,1,0:T(2,128)S(1)}, ...), condition=%wide.region_11.12_spmd.clone, body=%wide.region_9.11_spmd.clone.sunk | while | flops 1084756224 | bytes 25525972 | solution.py:244
  868.5 89.1 %while.65 = (s32[]{:T(128)}, f32[1,256,8,2,128]{1,4,3,2,0:T(8,128)S(1)}, bf16[1,2048,1024]{2,1,0:T(8,128)(2,1)}, bf16[1,2048,1024]{1,2,0:T(8,128)(2,1)}, bf16[1,...) while((s32[]{:T(128)}, ...), condition=%wide.region_13.14_spmd.clone, body=%wide.region_12.13_spmd.clone.sunk | while | flops 2708472064 | bytes 87490392 | solution.py:280
  961.3 6.2 convolution_convert_fusion.1
  967.5 12.5 copy.152
  980.1 7.1 convolution_convert_fusion.2
  987.2 12.3 copy.155
  999.5 16.6 convolution_convert_fusion
  1016.1 55.5 %reshape.1478 = bf16[2048,8192]{1,0:T(8,128)(2,1)} reshape(bf16[8192,2048]{1,0:T(8,128)(2,1)} %convolution_convert_fusion) | data formatting | bytes 67108864 | tf_op jit(solution)/shard_map/reshape | solution.py:74
  1071.6 8.4 constant_dynamic-update-slice_fusion.6
  1086.8 6.4 copy.153
  1097.6 6.6 copy.154
  1111.6 8.4 constant_dynamic-update-slice_fusion.3
  1120.1 16.1 convert_dynamic-update-slice_fusion.1
  1136.2 14.1 convert_dynamic-update-slice_fusion
  1150.3 23.0 constant_dynamic-update-slice_fusion.2
  1173.3 674.1 %reduce-scatter.10.cloned.1.call-done = bf16[256,30720]{1,0:T(8,128)(2,1)} async-done(((bf16[2048,30720]{1,0:T(8,128)(2,1)}), bf16[256,30720]{1,0:T(8,128)(2,1)}) %reduce-scatter.10.cloned.1.call-update) | async-done | bytes 15728656
  1850.9 7.3 fusion.112
  1858.2 16.7 fusion.56
  1882.7 51.4 %psum.15 = f32[2,2048]{1,0:T(2,128)S(1)} all-reduce(f32[2,2048]{1,0:T(2,128)S(1)} %pad_maximum_fusion.3), channel_id=1, replica_groups=mesh['grp'=8,'rep'=4] {'grp','rep'}, use_global_device_ids=true, to_apply=%region_21.22 | all-reduce | flops 4096 | bytes 32768 | tf_op jit(solution)/shard_map/psum | solution.py:331
  1938.0 440.7 %all-reduce.3.cloned.1.call-done = bf16[256,30720]{1,0:T(8,128)(2,1)} async-done(((bf16[256,30720]{1,0:T(8,128)(2,1)}), bf16[256,30720]{1,0:T(8,128)(2,1)}) %all-reduce.3.cloned.1.call-update) | async-done | bytes 15728656 | tf_op jit(solution)/shard_map/psum | solution.py:330
  2378.7 11.7 fusion.102
  2390.4 9.8 reshape.1479
  (344 shorter events, 257.4 us)
Async XLA Ops:
  7.2 58.0 %copy-start = (s32[1,2048]{1,0:T(1,128)S(1)}, s32[1,2048]{1,0:T(1,128)}, u32[]{:S(2)}) copy-start(s32[1,2048]{1,0:T(1,128)} %param.24) | copy-start | bytes 24580
  7.2 42.2 %all-gather.12.cloned.1.call-start = ((), (), s32[]{:S(2)}) async-start(), calls=%async_computation.3 | async-start | bytes 4718592 | tf_op jit(solution)/shard_map/all_gather | solution.py:127
  7.9 80.1 %all-gather.14.cloned.1.call-start = ((), (), s32[]{:S(2)}) async-start(), calls=%async_computation.4 | async-start | bytes 4718592 | tf_op jit(solution)/shard_map/all_gather | solution.py:126
  8.7 118.5 %all-gather.26.cloned.1.call-start = ((), (), s32[]{:S(2)}) async-start(), calls=%async_computation.13 | async-start | bytes 4718592 | tf_op jit(solution)/shard_map/all_gather | solution.py:145
  10.2 44.2 %copy-start.41 = (s32[1,16]{1,0:T(1,128)S(1)}, s32[1,16]{1,0:T(1,128)}, u32[]{:S(2)}) copy-start(s32[1,16]{1,0:T(1,128)} %param.23) | copy-start | bytes 196
  10.3 212.2 %copy-start.42 = (f32[256]{0:T(256)}, f32[256]{0:T(256)S(1)}, u32[]{:S(2)}) copy-start(f32[256]{0:T(256)S(1)} %add_rsqrt_fusion.1) | copy-start | bytes 3076
  54.0 112.3 %all-gather.28.cloned.1.call-start = ((), (), s32[]{:S(2)}) async-start(), calls=%async_computation.14 | async-start | bytes 4718592 | tf_op jit(solution)/shard_map/all_gather | solution.py:142
  65.2 22.8 copy-start.6
  65.2 22.8 copy-start.38
  77.4 152.3 %copy-start.26 = (f32[256,128]{0,1:T(8,128)}, f32[256,128]{0,1:T(8,128)S(1)}, u32[]{:S(2)}) copy-start(f32[256,128]{0,1:T(8,128)S(1)} %get-tuple-element.1233) | copy-start | bytes 393220
  77.4 152.3 %copy-start.29 = (f32[256,128]{0,1:T(8,128)}, f32[256,128]{0,1:T(8,128)S(1)}, u32[]{:S(2)}) copy-start(f32[256,128]{0,1:T(8,128)S(1)} %get-tuple-element.1234) | copy-start | bytes 393220
  77.5 14.9 copy-start.33
  77.7 14.8 copy-start.31
  94.9 127.6 %all-gather.16.cloned.1.call-start = ((), (), s32[]{:S(2)}) async-start(), calls=%async_computation.5 | async-start | bytes 9437184 | tf_op jit(solution)/shard_map/all_gather | solution.py:125
  95.5 221.8 %all-gather.18.cloned.1.call-start = ((), (), s32[]{:S(2)}) async-start(), calls=%async_computation.6 | async-start | bytes 9437184 | tf_op jit(solution)/shard_map/all_gather | solution.py:128
  96.0 345.3 %all-gather.20.cloned.1.call-start = ((), (), s32[]{:S(2)}) async-start(), calls=%async_computation.7 | async-start | bytes 37748736 | tf_op jit(solution)/shard_map/all_gather | solution.py:203
  96.8 507.2 %all-gather.22.cloned.1.call-start = ((), (), s32[]{:S(2)}) async-start(), calls=%async_computation.8 | async-start | bytes 37748736 | tf_op jit(solution)/shard_map/all_gather | solution.py:204
  97.5 669.2 %all-gather.24.cloned.1.call-start = ((), (), s32[]{:S(2)}) async-start(), calls=%async_computation.9 | async-start | bytes 37748736 | tf_op jit(solution)/shard_map/all_gather | solution.py:212
  98.3 981.7 %reduce-scatter.6.cloned.1.call-start = ((), (), s32[]{:S(2)}) async-start(), calls=%async_computation.10 | async-start | bytes 4718592 | tf_op jit(solution)/shard_map/reduce_scatter | solution.py:284
  317.3 6.3 copy-start.17
  317.3 7.6 copy-start.44
  325.1 278.9 %copy-start.35 = (bf16[256,2048]{1,0:T(8,128)(2,1)}, bf16[256,2048]{1,0:T(8,128)(2,1)S(1)}, u32[]{:S(2)}) copy-start(bf16[256,2048]{1,0:T(8,128)(2,1)S(1)} %multiply_convert_fusion.3) | copy-start | bytes 3145732
  461.5 305.2 %copy-start.21 = (bf16[1,256,2048]{2,1,0:T(8,128)(2,1)S(1)}, bf16[1,256,2048]{2,1,0:T(8,128)(2,1)}, u32[]{:S(2)}) copy-start(bf16[1,256,2048]{2,1,0:T(8,128)(2,1)} %param.22) | copy-start | bytes 3145732
  789.9 17.0 copy-start.14
  863.4 5.1 copy-start.3
  882.0 3.4 copy-start.2
  882.0 3.7 copy-start.9
  904.3 3.4 copy-start.2
  904.3 3.7 copy-start.9
  926.6 3.7 copy-start.9
  948.8 3.7 copy-start.9
  957.6 135.6 %reduce-scatter.8.cloned.1.call-start = ((), (), s32[]{:S(2)}) async-start(), calls=%async_computation.11 | async-start | bytes 4718592 | tf_op jit(solution)/shard_map/reduce_scatter | solution.py:287
  958.4 889.1 %reduce-scatter.10.cloned.1.call-start = ((), (), s32[]{:S(2)}) async-start(), calls=%async_computation.15 | async-start | bytes 141557760
  967.5 12.6 copy-start.11
  987.2 12.3 copy-start.22
  1071.6 9.8 copy-start.34
  1104.3 4.9 copy-start.16
  1111.6 8.4 copy-start.36
  1120.1 16.1 copy-start.46
  1173.3 1205.4 %all-reduce.3.cloned.1.call-start = ((), (), s32[]{:S(2)}) async-start(), calls=%async_computation.12 | async-start | bytes 31457280 | tf_op jit(solution)/shard_map/psum | solution.py:330
  1850.9 7.3 copy-start.15
  1850.9 7.3 copy-start.20
  1858.2 16.7 copy-start.19
  1858.2 16.7 copy-start.24
  1875.0 4.6 copy-start.23
  1875.0 4.6 copy-start.25
  1879.6 55.1 %copy-start.12 = (f32[256,2048]{1,0:T(8,128)S(1)}, f32[256,2048]{1,0:T(8,128)}, u32[]{:S(2)}) copy-start(f32[256,2048]{1,0:T(8,128)} %copy-done.10) | copy-start | bytes 6291460
  2400.2 6.9 copy-start.1
  (21 other events, 43.9 us)
Sparse Core Ops, SparseCore 0:
  9.9 39.4 all-gather.11
  51.3 36.7 all-gather.13
  90.5 36.7 all-gather.25
  129.5 36.7 all-gather.27
  168.0 54.3 all-gather.15
  224.2 54.3 all-gather.17
  280.5 160.7 all-gather.19
  443.2 160.7 all-gather.21
  605.9 160.7 all-gather.23
  957.7 51.3 reduce-scatter.5
  1012.8 51.3 reduce-scatter.7
  1173.4 673.9 reduce-scatter.9
  1850.0 528.6 all-reduce.2
where the time goes:
time: 2420 us; the launch traced here: 2410 us
  waiting for transfers between devices  1680 us (69%)
  matrix products  347 us (14%)
  local copies, waits for them, and re-layouts  262 us (11%)
  other arithmetic  54.5 us (2%)
  blocking collectives  51.4 us (2%)
    unnamed x14, waiting for transfers between devices  679 us
    psum x1, waiting for transfers between devices, on_device(): lax.psum(grad_shard.astype(jnp.bfloat16), 'rep').astype(jnp.float32)  441 us
    all_gather x1, waiting for transfers between devices, on_device(): lax.all_gather(w_down, 'grp', axis=0, tiled=True)  143 us
    all_gather x1, waiting for transfers between devices, on_device(): rows_up = lax.all_gather(w_up, 'grp', axis=0, tiled=True)  143 us
    all_gather x1, waiting for transfers between devices, on_device(): rows_gate = lax.all_gather(w_gate, 'grp', axis=0, tiled=True)  116 us
    dot_general x6, matrix products, matmul_f32(): return jnp.dot(first, second, preferred_element_type=jnp.float32)  71.5 us
    dot_general x7, matrix products, over_tokens(): jnp.einsum('tr,tc->rc', first, second, preferred_element_type=jnp.float32)  67.9 us
    dot_general x6, matrix products, against_rows(): jnp.einsum('tc,rc->tr', first, second, preferred_element_type=jnp.float32)  56.5 us
  transfers between devices with their start and end apart: 13, of which 10 were waited for; matrix products, arithmetic and copies ran while one was open for 15% of the time, Pallas kernels for 0%

commit v1 on v0

--- a/solution.py
+++ b/solution.py
@@ -327,7 +327,9 @@
         scatter_dimension=0,
         tiled=True,
     ).astype(jnp.float32)
-    grad_shard = lax.psum(grad_shard.astype(jnp.bfloat16), "rep").astype(jnp.float32)
+    grad_shard = jnp.sum(lax.all_gather(grad_shard.astype(jnp.bfloat16), "rep"), axis=0).astype(
+        jnp.float32
+    )
     gain_total = lax.psum(jnp.stack([gain_attn_term, gain_ffn_term]), ("grp", "rep"))
     own_gains = lax.dynamic_slice_in_dim(gain_total, own_index * rows_here, rows_here, 1)
     widths = [q_width, kv_width, kv_width, model_width, hidden_width, hidden_width, hidden_width]

time: 2420 us -> 2970 us (1.23)
  waiting for transfers between devices: 1680 us -> 2150 us
  blocking collectives: 51.4 us -> 83.1 us
    all_gather x0 -> x1, waiting for transfers between devices: none -> 913 us  [on_device(): lax.all_gather(grad_shard.astype(jnp.bfloat16), 'rep')]
    psum x1 -> x0, waiting for transfers between devices: 441 us -> none  [on_device(): lax.psum(grad_shard.astype(jnp.bfloat16), 'rep').astype(jnp.float32)]
    psum x1, blocking collectives: 51.4 us -> 83.1 us  [on_device(): lax.psum(jnp.stack([gain_attn_term, gain_ffn_term]), ('grp', 'rep'))]
  transfers between devices with their start and end apart: 13 -> 13, of which waited for: 10 -> 10; matrix products, arithmetic and copies ran while one was open for 15% -> 13% of each run, Pallas kernels for 0% -> 0%
where the time goes in v1:
time: 2970 us; the launch traced here: 2960 us
  waiting for transfers between devices  2150 us (72%)
  matrix products  357 us (12%)
  local copies, waits for them, and re-layouts  262 us (9%)
  other arithmetic  83.3 us (3%)
  blocking collectives  83.1 us (3%)
    all_gather x1, waiting for transfers between devices, on_device(): lax.all_gather(grad_shard.astype(jnp.bfloat16), 'rep')  913 us
    unnamed x14, waiting for transfers between devices  679 us
    all_gather x1, waiting for transfers between devices, on_device(): lax.all_gather(w_down, 'grp', axis=0, tiled=True)  143 us
    all_gather x1, waiting for transfers between devices, on_device(): rows_up = lax.all_gather(w_up, 'grp', axis=0, tiled=True)  143 us
    all_gather x1, waiting for transfers between devices, on_device(): rows_gate = lax.all_gather(w_gate, 'grp', axis=0, tiled=True)  116 us
    psum x1, blocking collectives, on_device(): lax.psum(jnp.stack([gain_attn_term, gain_ffn_term]), ('grp', 'rep'))  83.1 us
    dot_general x6, matrix products, matmul_f32(): return jnp.dot(first, second, preferred_element_type=jnp.float32)  80.9 us
    dot_general x7, matrix products, over_tokens(): jnp.einsum('tr,tc->rc', first, second, preferred_element_type=jnp.float32)  67.9 us
  transfers between devices with their start and end apart: 13, of which 10 were waited for; matrix products, arithmetic and copies ran while one was open for 13% of the time, Pallas kernels for 0%

profile of v1, /device:TPU:0, one launch (start us, length us, event | category | flops | bytes accessed | tf_op | source)
XLA Modules:
  0.0 2956.4 jit_solution(16926260441438193910)
XLA Ops:
  10.3 39.1 %all-gather.14.cloned.1.call-done = bf16[2048,1024]{1,0:T(8,128)(2,1)} async-done(((bf16[256,1024]{1,0:T(8,128)(2,1)}), bf16[2048,1024]{1,0:T(8,128)(2,1)}) %all-gather.14.cloned.1.call-update) | async-done | bytes 4194320 | tf_op jit(solution)/shard_map/all_gather | solution.py:127
  65.2 11.8 gather_fusion
  77.7 10.3 all-gather.16.cloned.1.call-done
  98.7 28.6 all-gather.28.cloned.1.call-done
  127.2 6.4 copy.139
  133.7 32.6 %all-gather.30.cloned.1.call-done = bf16[2048,1024]{1,0:T(8,128)(2,1)} async-done(((bf16[256,1024]{1,0:T(8,128)(2,1)}), bf16[2048,1024]{1,0:T(8,128)(2,1)}) %all-gather.30.cloned.1.call-update) | async-done | bytes 4194320 | tf_op jit(solution)/shard_map/all_gather | solution.py:142
  166.3 6.5 copy.140
  172.8 49.6 %all-gather.18.cloned.1.call-done = bf16[2048,2048]{1,0:T(8,128)(2,1)} async-done(((bf16[256,2048]{1,0:T(8,128)(2,1)}), bf16[2048,2048]{1,0:T(8,128)(2,1)}) %all-gather.18.cloned.1.call-update) | async-done | bytes 8388624 | tf_op jit(solution)/shard_map/all_gather | solution.py:125
  222.5 7.1 fusion.95
  231.1 47.8 %while.62 = (s32[]{:T(128)}, f32[1,8,2,256]{3,2,1,0:T(2,128)S(1)}, f32[1,8,2,256]{3,2,1,0:T(2,128)S(1)}, s32[1,2048]{1,0:T(1,128)S(1)}, s32[1,256]{1,0:T(1,128)S...) while((s32[]{:T(128)}, f32[1,8,2,256]{3,2,1,0:T(2,128)S(1)}, ...), condition=%wide.region_4.5_spmd.clone, body=%wide.region_1.4_spmd.clone.sunk | while | flops 552096000 | bytes 21593796 | solution.py:183
  249.5 5.8 exponential_reduce_fusion.2
  278.9 36.7 %while.63 = (s32[]{:T(128)}, f32[1,256,8,2,128]{1,4,3,2,0:T(8,128)}, bf16[1,2048,1024]{1,2,0:T(8,128)(2,1)}, s32[1,2048]{1,0:T(1,128)S(1)}, s32[1,256]{1,0:T(1,1...) while((s32[]{:T(128)}, ...), condition=%wide.region_6.7_spmd.clone, body=%wide.region_5.6_spmd.clone.sunk | while | flops 1083703552 | bytes 11828941 | solution.py:195
  290.6 6.6 bitcast_add_fusion.10
  300.1 6.1 bitcast_add_fusion.10
  309.1 6.1 bitcast_add_fusion.10
  317.4 6.2 multiply_reduce_fusion.2
  325.3 116.1 %all-gather.22.cloned.1.call-done = bf16[2048,8192]{1,0:T(8,128)(2,1)} async-done(((bf16[256,8192]{1,0:T(8,128)(2,1)}), bf16[2048,8192]{1,0:T(8,128)(2,1)}) %all-gather.22.cloned.1.call-update) | async-done | bytes 33554448 | tf_op jit(solution)/shard_map/all_gather | solution.py:203
  441.3 20.2 fusion.109
  461.5 142.5 %all-gather.24.cloned.1.call-done = bf16[2048,8192]{1,0:T(8,128)(2,1)} async-done(((bf16[256,8192]{1,0:T(8,128)(2,1)}), bf16[2048,8192]{1,0:T(8,128)(2,1)}) %all-gather.24.cloned.1.call-update) | async-done | bytes 33554448 | tf_op jit(solution)/shard_map/all_gather | solution.py:204
  604.0 20.2 fusion.110
  624.2 142.5 %all-gather.26.cloned.1.call-done = bf16[8192,2048]{1,0:T(8,128)(2,1)} async-done(((bf16[1024,2048]{1,0:T(8,128)(2,1)}), bf16[8192,2048]{1,0:T(8,128)(2,1)}) %all-gather.26.cloned.1.call-update) | async-done | bytes 33554448 | tf_op jit(solution)/shard_map/all_gather | solution.py:212
  766.8 23.2 multiply_convert_fusion
  790.0 17.0 fusion.111
  807.0 18.8 multiply_reduce_fusion
  829.6 5.8 convolution_convert_fusion.5
  838.6 24.8 while.64
  868.5 89.1 %while.65 = (s32[]{:T(128)}, f32[1,256,8,2,128]{1,4,3,2,0:T(8,128)S(1)}, bf16[1,2048,1024]{2,1,0:T(8,128)(2,1)}, bf16[1,2048,1024]{1,2,0:T(8,128)(2,1)}, bf16[1,...) while((s32[]{:T(128)}, ...), condition=%wide.region_13.14_spmd.clone, body=%wide.region_12.13_spmd.clone.sunk | while | flops 2708472064 | bytes 87490392 | solution.py:280
  961.3 6.2 convolution_convert_fusion.1
  967.5 12.5 copy.152
  980.1 7.1 convolution_convert_fusion.2
  987.2 12.3 copy.155
  999.5 16.6 convolution_convert_fusion
  1016.1 55.6 %reshape.1478 = bf16[2048,8192]{1,0:T(8,128)(2,1)} reshape(bf16[8192,2048]{1,0:T(8,128)(2,1)} %convolution_convert_fusion) | data formatting | bytes 67108864 | tf_op jit(solution)/shard_map/reshape | solution.py:74
  1071.6 8.4 constant_dynamic-update-slice_fusion.6
  1086.8 6.4 copy.153
  1097.7 6.6 copy.154
  1111.6 8.4 constant_dynamic-update-slice_fusion.3
  1120.1 16.1 convert_dynamic-update-slice_fusion.1
  1136.2 14.1 convert_dynamic-update-slice_fusion
  1150.3 23.0 constant_dynamic-update-slice_fusion.2
  1173.3 674.1 %reduce-scatter.10.cloned.1.call-done = bf16[256,30720]{1,0:T(8,128)(2,1)} async-done(((bf16[2048,30720]{1,0:T(8,128)(2,1)}), bf16[256,30720]{1,0:T(8,128)(2,1)}) %reduce-scatter.10.cloned.1.call-update) | async-done | bytes 15728656
  1850.9 7.3 fusion.112
  1858.3 26.1 fusion.56
  1893.0 83.1 %psum.7 = f32[2,2048]{1,0:T(2,128)S(1)} all-reduce(f32[2,2048]{1,0:T(2,128)S(1)} %pad_maximum_fusion.3), channel_id=1, replica_groups=mesh['grp'=8,'rep'=4] {'grp','rep'}, use_global_device_ids=true, to_apply=%region_21.22 | all-reduce | flops 4096 | bytes 32768 | tf_op jit(solution)/shard_map/psum | solution.py:333
  1980.0 912.5 %all-gather.32.cloned.1.call-done = bf16[1024,30720]{1,0:T(8,128)(2,1)} async-done(((bf16[256,30720]{1,0:T(8,128)(2,1)}), bf16[1024,30720]{1,0:T(8,128)(2,1)}) %all-gather.32.cloned.1.call-update) | async-done | bytes 62914576 | tf_op jit(solution)/shard_map/all_gather | solution.py:330
  2892.5 28.8 reduce_sum.96
  2928.1 11.7 fusion.102
  2939.9 9.8 reshape.1479
  (345 shorter events, 263.8 us)
Async XLA Ops:
  7.2 58.0 %copy-start = (s32[1,2048]{1,0:T(1,128)S(1)}, s32[1,2048]{1,0:T(1,128)}, u32[]{:S(2)}) copy-start(s32[1,2048]{1,0:T(1,128)} %param.24) | copy-start | bytes 24580
  7.2 42.2 %all-gather.14.cloned.1.call-start = ((), (), s32[]{:S(2)}) async-start(), calls=%async_computation.3 | async-start | bytes 4718592 | tf_op jit(solution)/shard_map/all_gather | solution.py:127
  7.9 80.1 %all-gather.16.cloned.1.call-start = ((), (), s32[]{:S(2)}) async-start(), calls=%async_computation.4 | async-start | bytes 4718592 | tf_op jit(solution)/shard_map/all_gather | solution.py:126
  8.7 118.5 %all-gather.28.cloned.1.call-start = ((), (), s32[]{:S(2)}) async-start(), calls=%async_computation.12 | async-start | bytes 4718592 | tf_op jit(solution)/shard_map/all_gather | solution.py:145
  10.2 44.2 %copy-start.41 = (s32[1,16]{1,0:T(1,128)S(1)}, s32[1,16]{1,0:T(1,128)}, u32[]{:S(2)}) copy-start(s32[1,16]{1,0:T(1,128)} %param.23) | copy-start | bytes 196
  10.3 212.2 %copy-start.42 = (f32[256]{0:T(256)}, f32[256]{0:T(256)S(1)}, u32[]{:S(2)}) copy-start(f32[256]{0:T(256)S(1)} %add_rsqrt_fusion.1) | copy-start | bytes 3076
  54.0 112.3 %all-gather.30.cloned.1.call-start = ((), (), s32[]{:S(2)}) async-start(), calls=%async_computation.13 | async-start | bytes 4718592 | tf_op jit(solution)/shard_map/all_gather | solution.py:142
  65.2 22.8 copy-start.6
  65.2 22.8 copy-start.38
  77.4 152.3 %copy-start.26 = (f32[256,128]{0,1:T(8,128)}, f32[256,128]{0,1:T(8,128)S(1)}, u32[]{:S(2)}) copy-start(f32[256,128]{0,1:T(8,128)S(1)} %get-tuple-element.1233) | copy-start | bytes 393220
  77.4 152.3 %copy-start.29 = (f32[256,128]{0,1:T(8,128)}, f32[256,128]{0,1:T(8,128)S(1)}, u32[]{:S(2)}) copy-start(f32[256,128]{0,1:T(8,128)S(1)} %get-tuple-element.1234) | copy-start | bytes 393220
  77.5 14.9 copy-start.33
  77.7 14.8 copy-start.31
  94.9 127.6 %all-gather.18.cloned.1.call-start = ((), (), s32[]{:S(2)}) async-start(), calls=%async_computation.5 | async-start | bytes 9437184 | tf_op jit(solution)/shard_map/all_gather | solution.py:125
  95.5 222.0 %all-gather.20.cloned.1.call-start = ((), (), s32[]{:S(2)}) async-start(), calls=%async_computation.6 | async-start | bytes 9437184 | tf_op jit(solution)/shard_map/all_gather | solution.py:128
  96.0 345.3 %all-gather.22.cloned.1.call-start = ((), (), s32[]{:S(2)}) async-start(), calls=%async_computation.7 | async-start | bytes 37748736 | tf_op jit(solution)/shard_map/all_gather | solution.py:203
  96.8 507.3 %all-gather.24.cloned.1.call-start = ((), (), s32[]{:S(2)}) async-start(), calls=%async_computation.8 | async-start | bytes 37748736 | tf_op jit(solution)/shard_map/all_gather | solution.py:204
  97.5 669.2 %all-gather.26.cloned.1.call-start = ((), (), s32[]{:S(2)}) async-start(), calls=%async_computation.9 | async-start | bytes 37748736 | tf_op jit(solution)/shard_map/all_gather | solution.py:212
  98.3 981.8 %reduce-scatter.6.cloned.1.call-start = ((), (), s32[]{:S(2)}) async-start(), calls=%async_computation.10 | async-start | bytes 4718592 | tf_op jit(solution)/shard_map/reduce_scatter | solution.py:284
  317.4 6.3 copy-start.17
  317.4 7.6 copy-start.44
  325.2 278.8 %copy-start.35 = (bf16[256,2048]{1,0:T(8,128)(2,1)}, bf16[256,2048]{1,0:T(8,128)(2,1)S(1)}, u32[]{:S(2)}) copy-start(bf16[256,2048]{1,0:T(8,128)(2,1)S(1)} %multiply_convert_fusion.3) | copy-start | bytes 3145732
  461.5 305.2 %copy-start.21 = (bf16[1,256,2048]{2,1,0:T(8,128)(2,1)S(1)}, bf16[1,256,2048]{2,1,0:T(8,128)(2,1)}, u32[]{:S(2)}) copy-start(bf16[1,256,2048]{2,1,0:T(8,128)(2,1)} %param.22) | copy-start | bytes 3145732
  789.9 17.0 copy-start.14
  863.4 5.1 copy-start.3
  882.0 3.4 copy-start.2
  882.0 3.7 copy-start.9
  904.3 3.7 copy-start.9
  926.6 3.4 copy-start.2
  926.6 3.7 copy-start.9
  948.8 3.7 copy-start.9
  957.6 135.6 %reduce-scatter.8.cloned.1.call-start = ((), (), s32[]{:S(2)}) async-start(), calls=%async_computation.11 | async-start | bytes 4718592 | tf_op jit(solution)/shard_map/reduce_scatter | solution.py:287
  958.4 889.1 %reduce-scatter.10.cloned.1.call-start = ((), (), s32[]{:S(2)}) async-start(), calls=%async_computation.15 | async-start | bytes 141557760
  967.5 12.6 copy-start.11
  987.2 12.3 copy-start.22
  1071.6 9.8 copy-start.34
  1104.3 4.9 copy-start.16
  1111.6 8.4 copy-start.36
  1120.1 16.1 copy-start.46
  1173.3 1719.3 %all-gather.32.cloned.1.call-start = ((), (), s32[]{:S(2)}) async-start(), calls=%async_computation.14 | async-start | bytes 78643200 | tf_op jit(solution)/shard_map/all_gather | solution.py:330
  1850.9 7.4 copy-start.15
  1850.9 7.4 copy-start.20
  1858.3 26.2 copy-start.19
  1858.3 26.2 copy-start.24
  1884.4 5.3 copy-start.23
  1884.4 5.5 copy-start.25
  1889.9 86.8 %copy-start.12 = (f32[256,2048]{1,0:T(8,128)S(1)}, f32[256,2048]{1,0:T(8,128)}, u32[]{:S(2)}) copy-start(f32[256,2048]{1,0:T(8,128)} %copy-done.10) | copy-start | bytes 6291460
  2939.9 9.8 copy-start.1
  (21 other events, 43.9 us)
Sparse Core Ops, SparseCore 0:
  9.9 39.4 all-gather.13
  51.3 36.7 all-gather.15
  90.5 36.7 all-gather.27
  129.5 36.7 all-gather.29
  168.0 54.3 all-gather.17
  224.2 54.3 all-gather.19
  280.5 160.7 all-gather.21
  443.2 160.7 all-gather.23
  605.9 160.7 all-gather.25
  957.7 51.3 reduce-scatter.5
  1012.8 51.3 reduce-scatter.7
  1173.4 673.9 reduce-scatter.9
  1849.1 1043.3 all-gather.31
